TPU v7x, 32 devices: a whole 2x2x4 slice. The times are simulated.
32 devices in a mesh: lon: 8 (over z, y), lat: 4 (over x, core).
Axes of the slice: x: 2, y: 2, z: 4, core: 2. Of those that a mesh axis runs over, the one named last changes fastest.
Arguments:
- ocean_state: float32 [4, 6, 768, 1024], P(None, None, 'lat', 'lon'), may hold values from -4 to 4
- sea_mask: int32 [6, 768, 1024], P(None, 'lat', 'lon'), may hold values 0 or 1
Outputs:
- new_state: float32 [4, 6, 768, 1024], P(None, None, 'lat', 'lon')
All inputs are finite; a program needn't handle non-finite values. No bound on the sum of `sea_mask` on one device may be relied on, other than what follows from the above.
Results may differ from a plain program's by a relative error of at most 0.00002.
Values sent between devices are 32-bit elements; how exact they have to be, the bound alone decides.
A program may use at most 128 MiB of HBM per device.

v0:
```python
import jax
import jax.numpy as jnp
from jax import lax
from jax.sharding import PartitionSpec as P

STEPS = 2


time_step = 0.1
thermal_coef = 0.2
haline_coef = 0.8
gravity = 0.5
spreading_coefficient = 0.05
viscosity = 0.05
coriolis_base = -0.6
coriolis_slope = 1.2


def partner(value, axis, stride):
    mask = 2**stride
    pairs = [(source, source ^ mask) for source in range(lax.axis_size(axis))]
    return lax.ppermute(value, axis, pairs)


def extended(cells, sides, width):
    for axis, dim in sides:
        count = lax.axis_size(axis)
        head = lax.slice_in_dim(cells, 0, width, axis=dim)
        tail = lax.slice_in_dim(cells, cells.shape[dim] - width, cells.shape[dim], axis=dim)
        cells = jnp.concatenate(
            [
                lax.ppermute(tail, axis, [(i, (i + 1) % count) for i in range(count)]),
                cells,
                lax.ppermute(head, axis, [((i + 1) % count, i) for i in range(count)]),
            ],
            axis=dim,
        )
    return cells


def east_diff(field):
    centre = field[..., 2:-2, :]
    return (
        8.0 * (centre[..., 3:-1] - centre[..., 1:-3]) - (centre[..., 4:] - centre[..., :-4])
    ) / 12.0


def north_diff(field):
    centre = field[..., 2:-2]
    return (
        8.0 * (centre[..., 3:-1, :] - centre[..., 1:-3, :])
        - (centre[..., 4:, :] - centre[..., :-4, :])
    ) / 12.0


def second_derivative_sum(field):
    centre = field[..., 2:-2, 2:-2]
    return (
        field[..., 3:-1, 2:-2]
        + field[..., 1:-3, 2:-2]
        + field[..., 2:-2, 3:-1]
        + field[..., 2:-2, 1:-3]
        - 4.0 * centre
    )


def full_tendency(bordered_grid_values, pressure, coriolis, water_indicator):
    heat_distribution, brine_concentration, eastward_current, northward_current = (
        bordered_grid_values[0],
        bordered_grid_values[1],
        bordered_grid_values[2],
        bordered_grid_values[3],
    )
    u_centre = eastward_current[..., 2:-2, 2:-2]
    v_centre = northward_current[..., 2:-2, 2:-2]

    def kept_prior_values(field):
        return -(u_centre * east_diff(field) + v_centre * north_diff(field))

    heat_increment = kept_prior_values(
        heat_distribution
    ) + spreading_coefficient * second_derivative_sum(heat_distribution)
    brine_increment = kept_prior_values(
        brine_concentration
    ) + spreading_coefficient * second_derivative_sum(brine_concentration)
    eastward_gradient = (
        kept_prior_values(eastward_current)
        + coriolis * v_centre
        - east_diff(pressure)
        + viscosity * second_derivative_sum(eastward_current)
    )
    northward_gradient = (
        kept_prior_values(northward_current)
        - coriolis * u_centre
        - north_diff(pressure)
        + viscosity * second_derivative_sum(northward_current)
    )
    return (
        jnp.stack([heat_increment, brine_increment, eastward_gradient, northward_gradient])
        * water_indicator
    )


def close_rows(bordered_grid_values):
    lon_count = lax.axis_size("lon")
    lat_count = lax.axis_size("lat")
    band = lax.axis_index("lat")
    northern = bordered_grid_values[:, :, -4:-2, :]
    mirrored = northern
    for bit_index in range(lon_count.bit_length() - 1):
        mirrored = partner(mirrored, "lon", bit_index)
    signs = jnp.array([1.0, 1.0, -1.0, -1.0], jnp.float32)[:, None, None, None]
    ghost = mirrored[:, :, ::-1, ::-1] * signs
    upper = jnp.where(band == lat_count - 1, ghost, bordered_grid_values[:, :, -2:, :])
    lower = jnp.where(band == 0, jnp.zeros_like(ghost), bordered_grid_values[:, :, :2, :])
    return jnp.concatenate([lower, bordered_grid_values[:, :, 2:-2, :], upper], axis=2)


def section_padding(fields):
    bordered_grid_values = extended(fields, (("lon", 3), ("lat", 2)), 2)
    return close_rows(bordered_grid_values)


def apply_tendency(bordered_grid_values, coriolis, water_indicator):
    density = haline_coef * bordered_grid_values[1] - thermal_coef * bordered_grid_values[0]
    pressure = gravity * jnp.cumsum(density, axis=0)
    return full_tendency(bordered_grid_values, pressure, coriolis, water_indicator)


def shards(ocean_state, sea_mask):
    water_indicator = sea_mask.astype(jnp.float32)
    lat_rows = ocean_state.shape[2]
    total_rows = lat_rows * lax.axis_size("lat")
    rows = (lax.axis_index("lat") * lat_rows + jnp.arange(lat_rows)).astype(jnp.float32)
    coriolis = (coriolis_base + coriolis_slope * (rows + 0.5) / total_rows)[:, None]
    fields = ocean_state * water_indicator
    for repeat in range(STEPS):
        first = fields + time_step * apply_tendency(
            section_padding(fields), coriolis, water_indicator
        )
        second = 0.75 * fields + 0.25 * (
            first + time_step * apply_tendency(section_padding(first), coriolis, water_indicator)
        )
        fields = fields / 3.0 + 2.0 / 3.0 * (
            second + time_step * apply_tendency(section_padding(second), coriolis, water_indicator)
        )
    return fields


def solution(mesh):
    in_specs = (P(None, None, "lat", "lon"), P(None, "lat", "lon"))
    out_specs = P(None, None, "lat", "lon")
    return jax.shard_map(shards, mesh=mesh, in_specs=in_specs, out_specs=out_specs, check_vma=False)
```

profile of v0, /device:TPU:0, one launch (start us, length us, event | category | flops | bytes accessed | tf_op | source)
XLA Modules:
  0.0 305.5 jit_solution(3558684927841194266)
XLA Ops:
  32.9 3.6 %collective-permute-done.5 = f32[4,6,2,132]{3,2,1,0:T(2,128)S(1)} collective-permute-done((f32[4,6,2,132]{3,2,1,0:T(2,128)S(1)}, f32[4,6,2,132]{3,2,1,0:T(2,128)S(1)}, u32[]{:S(2)}, u32[]{:S(2)}) %collective-permute-start.5) | collective-permute-done | bytes 25376 | tf_op jit(solution)/shard_map/ppermute | solution.py:22
  37.1 4.1 %pad_maximum_fusion = f32[4,6,196,132]{3,2,1,0:T(8,128)S(1)} fusion(f32[4,6,2,132]{3,2,1,0:T(2,128)S(1)} %multiply_select_fusion.5, f32[4,6,192,2]{3,2,1,0:T(8,128)} %copy.49, f32[4,6,192,128]{3,2,1,0:T(8,128)S(1)} %broadcast_multiply_fusion, f32[4,6,192,2]{3,2,1,0:T(8,128)} %copy.48, f32[4,6,2,132]{3,2,1,0:T(2,128)S(1)} %broadcast_select_fusion.5), kind=kLoop, calls=%fused_computation | loop fusion | flops 2483712 | bytes 4967424 | tf_op jit(solution)/shard_map/concatenate | solution.py:116
  57.2 3.2 %copy.51 = f32[4,6,192,2]{2,0,3,1:T(4,128)} copy(f32[4,6,192,2]{3,2,1,0:T(8,128)} %get-tuple-element.50) | data formatting | bytes 73728 | tf_op jit(solution)/shard_map/slice | solution.py:28
  60.4 3.8 %collective-permute-start.8 = (f32[4,6,192,2]{2,0,3,1:T(4,128)}, f32[4,6,192,2]{2,0,3,1:T(4,128)}, u32[]{:S(2)}, u32[]{:S(2)}) collective-permute-start(f32[4,6,192,2]{2,0,3,1:T(4,128)} %copy.51), channel_id=1, source_target_pairs={{4,0},{8,4},{12,8},{16,12},{20,16},{24,20},{28,24},{0,28},{5,1},{9... | collective-permute-start | bytes 110600 | tf_op jit(solution)/shard_map/ppermute | solution.py:34
  72.0 4.1 %collective-permute-done.10 = f32[4,6,2,132]{3,2,1,0:T(2,128)S(1)} collective-permute-done((f32[4,6,2,132]{3,2,1,0:T(2,128)S(1)}, f32[4,6,2,132]{3,2,1,0:T(2,128)S(1)}, u32[]{:S(2)}, u32[]{:S(2)}) %collective-permute-start.10) | collective-permute-done | bytes 25376 | tf_op jit(solution)/shard_map/ppermute | solution.py:22
  82.1 3.5 %collective-permute-done.12 = f32[4,6,2,132]{3,2,1,0:T(2,128)} collective-permute-done((f32[4,6,2,132]{3,2,1,0:T(2,128)S(1)}, f32[4,6,2,132]{3,2,1,0:T(2,128)}, u32[]{:S(2)}, u32[]{:S(2)}) %collective-permute-start.12) | collective-permute-done | bytes 25376 | tf_op jit(solution)/shard_map/ppermute | solution.py:22
  88.2 4.1 %pad_maximum_fusion.1 = f32[4,6,196,132]{3,2,1,0:T(8,128)S(1)} fusion(f32[4,6,2,132]{3,2,1,0:T(2,128)S(1)} %multiply_select_fusion.4, f32[4,6,192,2]{3,2,1,0:T(8,128)} %copy.53, f32[4,6,192,128]{3,2,1,0:T(8,128)S(1)} %fusion.1, f32[4,6,192,2]{3,2,1,0:T(8,128)} %copy.52, f32[4,6,2,132]{3,2,1,0:T(2,128)} %broadcast_select_fusion.4), kind=kLoop, calls=%fused_computation.1 | loop fusion | flops 2483712 | bytes 4967424 | tf_op jit(solution)/shard_map/concatenate | solution.py:116
  108.0 3.2 %copy.55 = f32[4,6,192,2]{2,0,3,1:T(4,128)} copy(f32[4,6,192,2]{3,2,1,0:T(8,128)} %get-tuple-element.48) | data formatting | bytes 73728 | tf_op jit(solution)/shard_map/slice | solution.py:28
  111.2 4.6 %collective-permute-start.15 = (f32[4,6,192,2]{2,0,3,1:T(4,128)}, f32[4,6,192,2]{2,0,3,1:T(4,128)}, u32[]{:S(2)}, u32[]{:S(2)}) collective-permute-start(f32[4,6,192,2]{2,0,3,1:T(4,128)} %copy.55), channel_id=1, source_target_pairs={{4,0},{8,4},{12,8},{16,12},{20,16},{24,20},{28,24},{0,28},{5,1},{9... | collective-permute-start | bytes 110600 | tf_op jit(solution)/shard_map/ppermute | solution.py:34
  123.6 4.1 %collective-permute-done.17 = f32[4,6,2,132]{3,2,1,0:T(2,128)S(1)} collective-permute-done((f32[4,6,2,132]{3,2,1,0:T(2,128)S(1)}, f32[4,6,2,132]{3,2,1,0:T(2,128)S(1)}, u32[]{:S(2)}, u32[]{:S(2)}) %collective-permute-start.17) | collective-permute-done | bytes 25376 | tf_op jit(solution)/shard_map/ppermute | solution.py:22
  133.7 3.5 %collective-permute-done.19 = f32[4,6,2,132]{3,2,1,0:T(2,128)} collective-permute-done((f32[4,6,2,132]{3,2,1,0:T(2,128)S(1)}, f32[4,6,2,132]{3,2,1,0:T(2,128)}, u32[]{:S(2)}, u32[]{:S(2)}) %collective-permute-start.19) | collective-permute-done | bytes 25376 | tf_op jit(solution)/shard_map/ppermute | solution.py:22
  139.8 4.1 %pad_maximum_fusion.2 = f32[4,6,196,132]{3,2,1,0:T(8,128)S(1)} fusion(f32[4,6,2,132]{3,2,1,0:T(2,128)S(1)} %multiply_select_fusion.3, f32[4,6,192,2]{3,2,1,0:T(8,128)} %copy.57, f32[4,6,192,128]{3,2,1,0:T(8,128)S(1)} %fusion.5, f32[4,6,192,2]{3,2,1,0:T(8,128)} %copy.56, f32[4,6,2,132]{3,2,1,0:T(2,128)} %broadcast_select_fusion.3), kind=kLoop, calls=%fused_computation.2 | loop fusion | flops 2483712 | bytes 4967424 | tf_op jit(solution)/shard_map/concatenate | solution.py:116
  162.5 5.1 %collective-permute-start.22 = (f32[4,6,192,2]{2,0,3,1:T(4,128)S(1)}, f32[4,6,192,2]{2,0,3,1:T(4,128)S(1)}, u32[]{:S(2)}, u32[]{:S(2)}) collective-permute-start(f32[4,6,192,2]{2,0,3,1:T(4,128)S(1)} %copy.59), channel_id=1, source_target_pairs={{4,0},{8,4},{12,8},{16,12},{20,16},{24,20},{28,24},{0,28},{5,1},{9... | collective-permute-start | bytes 110600 | tf_op jit(solution)/shard_map/ppermute | solution.py:34
  173.3 4.1 %collective-permute-done.24 = f32[4,6,2,132]{3,2,1,0:T(2,128)S(1)} collective-permute-done((f32[4,6,2,132]{3,2,1,0:T(2,128)S(1)}, f32[4,6,2,132]{3,2,1,0:T(2,128)S(1)}, u32[]{:S(2)}, u32[]{:S(2)}) %collective-permute-start.24) | collective-permute-done | bytes 25376 | tf_op jit(solution)/shard_map/ppermute | solution.py:22
  183.2 3.8 %collective-permute-done.26 = f32[4,6,2,132]{3,2,1,0:T(2,128)S(1)} collective-permute-done((f32[4,6,2,132]{3,2,1,0:T(2,128)S(1)}, f32[4,6,2,132]{3,2,1,0:T(2,128)S(1)}, u32[]{:S(2)}, u32[]{:S(2)}) %collective-permute-start.26) | collective-permute-done | bytes 25376 | tf_op jit(solution)/shard_map/ppermute | solution.py:22
  187.5 4.1 %pad_maximum_fusion.3 = f32[4,6,196,132]{3,2,1,0:T(8,128)S(1)} fusion(f32[4,6,2,132]{3,2,1,0:T(2,128)S(1)} %multiply_select_fusion.2, f32[4,6,192,2]{3,2,1,0:T(8,128)} %copy.61, f32[4,6,192,128]{3,2,1,0:T(8,128)S(1)} %fusion.9, f32[4,6,192,2]{3,2,1,0:T(8,128)} %copy.60, f32[4,6,2,132]{3,2,1,0:T(2,128)S(1)} %broadcast_select_fusion.2), kind=kLoop, calls=%fused_computation.3 | loop fusion | flops 2483712 | bytes 4967424 | tf_op jit(solution)/shard_map/concatenate | solution.py:116
  210.0 4.6 %collective-permute-start.29 = (f32[4,6,192,2]{2,0,3,1:T(4,128)}, f32[4,6,192,2]{2,0,3,1:T(4,128)}, u32[]{:S(2)}, u32[]{:S(2)}) collective-permute-start(f32[4,6,192,2]{2,0,3,1:T(4,128)} %copy.63), channel_id=1, source_target_pairs={{4,0},{8,4},{12,8},{16,12},{20,16},{24,20},{28,24},{0,28},{5,1},{9... | collective-permute-start | bytes 110600 | tf_op jit(solution)/shard_map/ppermute | solution.py:34
  222.5 4.1 %collective-permute-done.31 = f32[4,6,2,132]{3,2,1,0:T(2,128)S(1)} collective-permute-done((f32[4,6,2,132]{3,2,1,0:T(2,128)S(1)}, f32[4,6,2,132]{3,2,1,0:T(2,128)S(1)}, u32[]{:S(2)}, u32[]{:S(2)}) %collective-permute-start.31) | collective-permute-done | bytes 25376 | tf_op jit(solution)/shard_map/ppermute | solution.py:22
  232.5 3.5 %collective-permute-done.33 = f32[4,6,2,132]{3,2,1,0:T(2,128)} collective-permute-done((f32[4,6,2,132]{3,2,1,0:T(2,128)S(1)}, f32[4,6,2,132]{3,2,1,0:T(2,128)}, u32[]{:S(2)}, u32[]{:S(2)}) %collective-permute-start.33) | collective-permute-done | bytes 25376 | tf_op jit(solution)/shard_map/ppermute | solution.py:22
  238.6 4.4 %pad_maximum_fusion.4 = f32[4,6,196,132]{3,2,1,0:T(8,128)S(1)} fusion(f32[4,6,2,132]{3,2,1,0:T(2,128)S(1)} %multiply_select_fusion.1, f32[4,6,192,2]{3,2,1,0:T(8,128)} %copy.65, f32[4,6,192,128]{3,2,1,0:T(8,128)} %copy-done.1, f32[4,6,192,2]{3,2,1,0:T(8,128)} %copy.64, f32[4,6,2,132]{3,2,1,0:T(2,128)} %broadcast_select_fusion.1), kind=kLoop, calls=%fused_computation.4 | loop fusion | flops 2483712 | bytes 4967424 | tf_op jit(solution)/shard_map/concatenate | solution.py:116
  261.3 4.9 %collective-permute-start.36 = (f32[4,6,192,2]{2,0,3,1:T(4,128)}, f32[4,6,192,2]{2,0,3,1:T(4,128)}, u32[]{:S(2)}, u32[]{:S(2)}) collective-permute-start(f32[4,6,192,2]{2,0,3,1:T(4,128)} %copy.67), channel_id=1, source_target_pairs={{4,0},{8,4},{12,8},{16,12},{20,16},{24,20},{28,24},{0,28},{5,1},{9... | collective-permute-start | bytes 110600 | tf_op jit(solution)/shard_map/ppermute | solution.py:34
  274.1 4.1 %collective-permute-done.38 = f32[4,6,2,132]{3,2,1,0:T(2,128)S(1)} collective-permute-done((f32[4,6,2,132]{3,2,1,0:T(2,128)S(1)}, f32[4,6,2,132]{3,2,1,0:T(2,128)S(1)}, u32[]{:S(2)}, u32[]{:S(2)}) %collective-permute-start.38) | collective-permute-done | bytes 25376 | tf_op jit(solution)/shard_map/ppermute | solution.py:22
  284.1 3.5 %collective-permute-done.40 = f32[4,6,2,132]{3,2,1,0:T(2,128)} collective-permute-done((f32[4,6,2,132]{3,2,1,0:T(2,128)S(1)}, f32[4,6,2,132]{3,2,1,0:T(2,128)}, u32[]{:S(2)}, u32[]{:S(2)}) %collective-permute-start.40) | collective-permute-done | bytes 25376 | tf_op jit(solution)/shard_map/ppermute | solution.py:22
  290.2 4.4 %pad_maximum_fusion.5 = f32[4,6,196,132]{3,2,1,0:T(8,128)S(1)} fusion(f32[4,6,2,132]{3,2,1,0:T(2,128)S(1)} %multiply_select_fusion, f32[4,6,192,2]{3,2,1,0:T(8,128)} %copy.69, f32[4,6,192,128]{3,2,1,0:T(8,128)} %copy-done, f32[4,6,192,2]{3,2,1,0:T(8,128)} %copy.68, f32[4,6,2,132]{3,2,1,0:T(2,128)} %broadcast_select_fusion), kind=kLoop, calls=%fused_computation.5 | loop fusion | flops 2483712 | bytes 4967424 | tf_op jit(solution)/shard_map/concatenate | solution.py:116
  (245 shorter events, 208.1 us)
Async XLA Ops:
  8.5 8.6 %collective-permute-start = (f32[4,6,192,2]{2,0,3,1:T(4,128)S(1)}, f32[4,6,192,2]{2,0,3,1:T(4,128)S(1)}, u32[]{:S(2)}, u32[]{:S(2)}) collective-permute-start(f32[4,6,192,2]{2,0,3,1:T(4,128)S(1)} %copy.46), channel_id=1, source_target_pairs={{0,4},{4,8},{8,12},{12,16},{16,20},{20,24},{24,28},{28,0},{1,5},{5... | collective-permute-start | bytes 110600 | tf_op jit(solution)/shard_map/ppermute | solution.py:32
  24.1 8.8 %collective-permute-start.2 = (f32[4,6,2,132]{3,2,1,0:T(2,128)S(1)}, f32[4,6,2,132]{3,2,1,0:T(2,128)S(1)}, u32[]{:S(2)}, u32[]{:S(2)}) collective-permute-start(f32[4,6,2,132]{3,2,1,0:T(2,128)S(1)} %get-tuple-element.15), channel_id=1, source_target_pairs={{0,1},{1,2},{2,3},{3,0},{4,5},{5,6},{6,7},{7,4},{8,9},{9,10},{10,1... | collective-permute-start | bytes 76040 | tf_op jit(solution)/shard_map/ppermute | solution.py:32
  27.8 9.1 %collective-permute-start.6 = (f32[4,6,2,132]{3,2,1,0:T(2,128)S(1)}, f32[4,6,2,132]{3,2,1,0:T(2,128)S(1)}, u32[]{:S(2)}, u32[]{:S(2)}) collective-permute-start(f32[4,6,2,132]{3,2,1,0:T(2,128)S(1)} %get-tuple-element.16), channel_id=1, source_target_pairs={{1,0},{2,1},{3,2},{0,3},{5,4},{6,5},{7,6},{4,7},{9,8},{10,9},{11,1... | collective-permute-start | bytes 76040 | tf_op jit(solution)/shard_map/ppermute | solution.py:34
  31.0 5.5 %collective-permute-start.5 = (f32[4,6,2,132]{3,2,1,0:T(2,128)S(1)}, f32[4,6,2,132]{3,2,1,0:T(2,128)S(1)}, u32[]{:S(2)}, u32[]{:S(2)}) collective-permute-start(f32[4,6,2,132]{3,2,1,0:T(2,128)S(1)} %collective-permute-done.4), channel_id=1, source_target_pairs={{0,16},{4,20},{8,24},{12,28},{16,0},{20,4},{24,8},{28,12},{1,17},{... | collective-permute-start | bytes 76040 | tf_op jit(solution)/shard_map/ppermute | solution.py:22
  56.3 7.9 %collective-permute-start.7 = (f32[4,6,192,2]{2,0,3,1:T(4,128)}, f32[4,6,192,2]{2,0,3,1:T(4,128)}, u32[]{:S(2)}, u32[]{:S(2)}) collective-permute-start(f32[4,6,192,2]{2,0,3,1:T(4,128)} %copy.50), channel_id=1, source_target_pairs={{0,4},{4,8},{8,12},{12,16},{16,20},{20,24},{24,28},{28,0},{1,5},{5... | collective-permute-start | bytes 110600 | tf_op jit(solution)/shard_map/ppermute | solution.py:32
  60.4 6.8 %collective-permute-start.8 = (f32[4,6,192,2]{2,0,3,1:T(4,128)}, f32[4,6,192,2]{2,0,3,1:T(4,128)}, u32[]{:S(2)}, u32[]{:S(2)}) collective-permute-start(f32[4,6,192,2]{2,0,3,1:T(4,128)} %copy.51), channel_id=1, source_target_pairs={{4,0},{8,4},{12,8},{16,12},{20,16},{24,20},{28,24},{0,28},{5,1},{9... | collective-permute-start | bytes 110600 | tf_op jit(solution)/shard_map/ppermute | solution.py:34
  76.1 5.4 %collective-permute-start.9 = (f32[4,6,2,132]{3,2,1,0:T(2,128)S(1)}, f32[4,6,2,132]{3,2,1,0:T(2,128)S(1)}, u32[]{:S(2)}, u32[]{:S(2)}) collective-permute-start(f32[4,6,2,132]{3,2,1,0:T(2,128)S(1)} %get-tuple-element.13), channel_id=1, source_target_pairs={{0,1},{1,2},{2,3},{3,0},{4,5},{5,6},{6,7},{7,4},{8,9},{9,10},{10,1... | collective-permute-start | bytes 76040 | tf_op jit(solution)/shard_map/ppermute | solution.py:32
  76.1 11.1 %collective-permute-start.13 = (f32[4,6,2,132]{3,2,1,0:T(2,128)}, f32[4,6,2,132]{3,2,1,0:T(2,128)}, u32[]{:S(2)}, u32[]{:S(2)}) collective-permute-start(f32[4,6,2,132]{3,2,1,0:T(2,128)} %get-tuple-element.14), channel_id=1, source_target_pairs={{1,0},{2,1},{3,2},{0,3},{5,4},{6,5},{7,6},{4,7},{9,8},{10,9},{11,1... | collective-permute-start | bytes 76040 | tf_op jit(solution)/shard_map/ppermute | solution.py:34
  80.2 5.4 %collective-permute-start.12 = (f32[4,6,2,132]{3,2,1,0:T(2,128)S(1)}, f32[4,6,2,132]{3,2,1,0:T(2,128)}, u32[]{:S(2)}, u32[]{:S(2)}) collective-permute-start(f32[4,6,2,132]{3,2,1,0:T(2,128)S(1)} %collective-permute-done.11), channel_id=1, source_target_pairs={{0,16},{4,20},{8,24},{12,28},{16,0},{20,4},{24,8},{28,12},{1,17},{... | collective-permute-start | bytes 76040 | tf_op jit(solution)/shard_map/ppermute | solution.py:22
  107.9 7.9 %collective-permute-start.14 = (f32[4,6,192,2]{2,0,3,1:T(4,128)}, f32[4,6,192,2]{2,0,3,1:T(4,128)}, u32[]{:S(2)}, u32[]{:S(2)}) collective-permute-start(f32[4,6,192,2]{2,0,3,1:T(4,128)} %copy.54), channel_id=1, source_target_pairs={{0,4},{4,8},{8,12},{12,16},{16,20},{20,24},{24,28},{28,0},{1,5},{5... | collective-permute-start | bytes 110600 | tf_op jit(solution)/shard_map/ppermute | solution.py:32
  111.2 7.6 %collective-permute-start.15 = (f32[4,6,192,2]{2,0,3,1:T(4,128)}, f32[4,6,192,2]{2,0,3,1:T(4,128)}, u32[]{:S(2)}, u32[]{:S(2)}) collective-permute-start(f32[4,6,192,2]{2,0,3,1:T(4,128)} %copy.55), channel_id=1, source_target_pairs={{4,0},{8,4},{12,8},{16,12},{20,16},{24,20},{28,24},{0,28},{5,1},{9... | collective-permute-start | bytes 110600 | tf_op jit(solution)/shard_map/ppermute | solution.py:34
  127.7 11.1 %collective-permute-start.20 = (f32[4,6,2,132]{3,2,1,0:T(2,128)}, f32[4,6,2,132]{3,2,1,0:T(2,128)}, u32[]{:S(2)}, u32[]{:S(2)}) collective-permute-start(f32[4,6,2,132]{3,2,1,0:T(2,128)} %get-tuple-element.12), channel_id=1, source_target_pairs={{1,0},{2,1},{3,2},{0,3},{5,4},{6,5},{7,6},{4,7},{9,8},{10,9},{11,1... | collective-permute-start | bytes 76040 | tf_op jit(solution)/shard_map/ppermute | solution.py:34
  131.8 5.4 %collective-permute-start.19 = (f32[4,6,2,132]{3,2,1,0:T(2,128)S(1)}, f32[4,6,2,132]{3,2,1,0:T(2,128)}, u32[]{:S(2)}, u32[]{:S(2)}) collective-permute-start(f32[4,6,2,132]{3,2,1,0:T(2,128)S(1)} %collective-permute-done.18), channel_id=1, source_target_pairs={{0,16},{4,20},{8,24},{12,28},{16,0},{20,4},{24,8},{28,12},{1,17},{... | collective-permute-start | bytes 76040 | tf_op jit(solution)/shard_map/ppermute | solution.py:22
  159.8 7.8 %collective-permute-start.21 = (f32[4,6,192,2]{2,0,3,1:T(4,128)S(1)}, f32[4,6,192,2]{2,0,3,1:T(4,128)S(1)}, u32[]{:S(2)}, u32[]{:S(2)}) collective-permute-start(f32[4,6,192,2]{2,0,3,1:T(4,128)S(1)} %copy.58), channel_id=1, source_target_pairs={{0,4},{4,8},{8,12},{12,16},{16,20},{20,24},{24,28},{28,0},{1,5},{5... | collective-permute-start | bytes 110600 | tf_op jit(solution)/shard_map/ppermute | solution.py:32
  162.5 7.3 %collective-permute-start.22 = (f32[4,6,192,2]{2,0,3,1:T(4,128)S(1)}, f32[4,6,192,2]{2,0,3,1:T(4,128)S(1)}, u32[]{:S(2)}, u32[]{:S(2)}) collective-permute-start(f32[4,6,192,2]{2,0,3,1:T(4,128)S(1)} %copy.59), channel_id=1, source_target_pairs={{4,0},{8,4},{12,8},{16,12},{20,16},{24,20},{28,24},{0,28},{5,1},{9... | collective-permute-start | bytes 110600 | tf_op jit(solution)/shard_map/ppermute | solution.py:34
  177.3 5.8 %collective-permute-start.23 = (f32[4,6,2,132]{3,2,1,0:T(2,128)S(1)}, f32[4,6,2,132]{3,2,1,0:T(2,128)S(1)}, u32[]{:S(2)}, u32[]{:S(2)}) collective-permute-start(f32[4,6,2,132]{3,2,1,0:T(2,128)S(1)} %get-tuple-element.9), channel_id=1, source_target_pairs={{0,1},{1,2},{2,3},{3,0},{4,5},{5,6},{6,7},{7,4},{8,9},{9,10},{10,1... | collective-permute-start | bytes 76040 | tf_op jit(solution)/shard_map/ppermute | solution.py:32
  177.3 10.0 %collective-permute-start.27 = (f32[4,6,2,132]{3,2,1,0:T(2,128)S(1)}, f32[4,6,2,132]{3,2,1,0:T(2,128)S(1)}, u32[]{:S(2)}, u32[]{:S(2)}) collective-permute-start(f32[4,6,2,132]{3,2,1,0:T(2,128)S(1)} %get-tuple-element.10), channel_id=1, source_target_pairs={{1,0},{2,1},{3,2},{0,3},{5,4},{6,5},{7,6},{4,7},{9,8},{10,9},{11,1... | collective-permute-start | bytes 76040 | tf_op jit(solution)/shard_map/ppermute | solution.py:34
  181.4 5.5 %collective-permute-start.26 = (f32[4,6,2,132]{3,2,1,0:T(2,128)S(1)}, f32[4,6,2,132]{3,2,1,0:T(2,128)S(1)}, u32[]{:S(2)}, u32[]{:S(2)}) collective-permute-start(f32[4,6,2,132]{3,2,1,0:T(2,128)S(1)} %collective-permute-done.25), channel_id=1, source_target_pairs={{0,16},{4,20},{8,24},{12,28},{16,0},{20,4},{24,8},{28,12},{1,17},{... | collective-permute-start | bytes 76040 | tf_op jit(solution)/shard_map/ppermute | solution.py:22
  206.5 8.1 %collective-permute-start.28 = (f32[4,6,192,2]{2,0,3,1:T(4,128)}, f32[4,6,192,2]{2,0,3,1:T(4,128)}, u32[]{:S(2)}, u32[]{:S(2)}) collective-permute-start(f32[4,6,192,2]{2,0,3,1:T(4,128)} %copy.62), channel_id=1, source_target_pairs={{0,4},{4,8},{8,12},{12,16},{16,20},{20,24},{24,28},{28,0},{1,5},{5... | collective-permute-start | bytes 110600 | tf_op jit(solution)/shard_map/ppermute | solution.py:32
  210.0 7.6 %collective-permute-start.29 = (f32[4,6,192,2]{2,0,3,1:T(4,128)}, f32[4,6,192,2]{2,0,3,1:T(4,128)}, u32[]{:S(2)}, u32[]{:S(2)}) collective-permute-start(f32[4,6,192,2]{2,0,3,1:T(4,128)} %copy.63), channel_id=1, source_target_pairs={{4,0},{8,4},{12,8},{16,12},{20,16},{24,20},{28,24},{0,28},{5,1},{9... | collective-permute-start | bytes 110600 | tf_op jit(solution)/shard_map/ppermute | solution.py:34
  226.6 11.1 %collective-permute-start.34 = (f32[4,6,2,132]{3,2,1,0:T(2,128)}, f32[4,6,2,132]{3,2,1,0:T(2,128)}, u32[]{:S(2)}, u32[]{:S(2)}) collective-permute-start(f32[4,6,2,132]{3,2,1,0:T(2,128)} %get-tuple-element.8), channel_id=1, source_target_pairs={{1,0},{2,1},{3,2},{0,3},{5,4},{6,5},{7,6},{4,7},{9,8},{10,9},{11,1... | collective-permute-start | bytes 76040 | tf_op jit(solution)/shard_map/ppermute | solution.py:34
  258.1 8.1 %collective-permute-start.35 = (f32[4,6,192,2]{2,0,3,1:T(4,128)}, f32[4,6,192,2]{2,0,3,1:T(4,128)}, u32[]{:S(2)}, u32[]{:S(2)}) collective-permute-start(f32[4,6,192,2]{2,0,3,1:T(4,128)} %copy.66), channel_id=1, source_target_pairs={{0,4},{4,8},{8,12},{12,16},{16,20},{20,24},{24,28},{28,0},{1,5},{5... | collective-permute-start | bytes 110600 | tf_op jit(solution)/shard_map/ppermute | solution.py:32
  261.3 7.9 %collective-permute-start.36 = (f32[4,6,192,2]{2,0,3,1:T(4,128)}, f32[4,6,192,2]{2,0,3,1:T(4,128)}, u32[]{:S(2)}, u32[]{:S(2)}) collective-permute-start(f32[4,6,192,2]{2,0,3,1:T(4,128)} %copy.67), channel_id=1, source_target_pairs={{4,0},{8,4},{12,8},{16,12},{20,16},{24,20},{28,24},{0,28},{5,1},{9... | collective-permute-start | bytes 110600 | tf_op jit(solution)/shard_map/ppermute | solution.py:34
  278.2 11.1 %collective-permute-start.41 = (f32[4,6,2,132]{3,2,1,0:T(2,128)}, f32[4,6,2,132]{3,2,1,0:T(2,128)}, u32[]{:S(2)}, u32[]{:S(2)}) collective-permute-start(f32[4,6,2,132]{3,2,1,0:T(2,128)} %get-tuple-element.6), channel_id=1, source_target_pairs={{1,0},{2,1},{3,2},{0,3},{5,4},{6,5},{7,6},{4,7},{9,8},{10,9},{11,1... | collective-permute-start | bytes 76040 | tf_op jit(solution)/shard_map/ppermute | solution.py:34
  (58 other events, 181.2 us)
where the time goes:
time: 310 us; the launch traced here: 305 us
  local copies, waits for them, and re-layouts  99.3 us (32%)
  other arithmetic  95.4 us (31%)
  waiting for transfers between devices  58.9 us (19%)
  starting transfers between devices  50.7 us (16%)
    ppermute x18, waiting for transfers between devices, partner(): return lax.ppermute(value, axis, pairs)  58.8 us
    another operation x24, other arithmetic, full_tendency(): jnp.stack([heat_increment, brine_increment, eastward_gradient, northward_...  43 us
    slice x12, local copies, waits for them, and re-layouts, extended(): lax.slice_in_dim(cells, cells.shape[dim] - width, cells.shape[dim], axis=...  35.9 us
    ppermute x12, starting transfers between devices, extended(): lax.ppermute(head, axis, [((i + 1) % count, i) for i in range(count)])  35.5 us
    concatenate x6, other arithmetic, close_rows(): jnp.concatenate([lower, bordered_grid_values[:, :, 2:-2, :], upper], axis=2)  25 us
    slice x6, local copies, waits for them, and re-layouts, extended(): head = lax.slice_in_dim(cells, 0, width, axis=dim)  17.9 us
    ppermute x6, local copies, waits for them, and re-layouts, extended(): lax.ppermute(head, axis, [((i + 1) % count, i) for i in range(count)])  16.2 us
    ppermute x6, local copies, waits for them, and re-layouts, extended(): lax.ppermute(tail, axis, [(i, (i + 1) % count) for i in range(count)])  16.2 us
  transfers between devices with their start and end apart: 42, of which 18 were waited for; matrix products, arithmetic and copies ran while one was open for 14% of the time, Pallas kernels for 0%

commit v1 on v0

v1 whole, which is shorter than its diff:
```python
import functools

import jax
import jax.numpy as jnp
from jax import lax
from jax.experimental import pallas as pl
from jax.experimental.pallas import tpu as pltpu
from jax.sharding import PartitionSpec as P

STEPS = 2
SUB = 8
LANE = 128
FIELDS = 4
CHUNK = 2

time_step = 0.1
thermal_coef = 0.2
haline_coef = 0.8
gravity = 0.5
spreading_coefficient = 0.05
coriolis_base = -0.6
coriolis_slope = 1.2

MESH = pl.DeviceIdType.MESH


def kernel(
    levels, rows, width, lon_n, lat_n,
    in_hbm, mask_hbm, out_hbm,
    fin, min_, fout, wet, q0, q1, q2,
    lon_out, lon_in, lat_out, lat_in,
    local_sem, lon_ssem, lon_rsem, lat_ssem, lat_rsem,
):
    items = FIELDS * levels
    run = rows // SUB
    positions = run // 2
    chunks = positions // CHUNK
    tiles = width // LANE
    lon = lax.axis_index("lon")
    lat = lax.axis_index("lat")
    east = lax.rem(lon + 1, lon_n)
    west = lax.rem(lon + lon_n - 1, lon_n)
    mirror = lon_n - 1 - lon

    loads = []
    for j in range(tiles):
        lanes = pl.ds(j * LANE, LANE)
        loads.append(pltpu.make_async_copy(mask_hbm.at[:, :, lanes], min_.at[j], local_sem.at[2 * j]))
        loads.append(pltpu.make_async_copy(in_hbm.at[:, :, :, lanes], fin.at[j], local_sem.at[2 * j + 1]))
    for copy in loads:
        copy.start()

    barrier = pltpu.get_barrier_semaphore()
    pl.semaphore_signal(barrier, inc=1, device_id={"lon": east}, device_id_type=MESH)
    pl.semaphore_signal(barrier, inc=1, device_id={"lon": west}, device_id_type=MESH)

    @pl.when(lat > 0)
    def _():
        pl.semaphore_signal(barrier, inc=1, device_id={"lat": lat - 1}, device_id_type=MESH)

    @pl.when(lat < lat_n - 1)
    def _():
        pl.semaphore_signal(barrier, inc=1, device_id={"lat": lat + 1}, device_id_type=MESH)

    @pl.when(lat == lat_n - 1)
    def _():
        pl.semaphore_signal(barrier, inc=1, device_id={"lon": mirror}, device_id_type=MESH)

    @pl.when(lat == 0)
    def _():
        lat_in[0] = jnp.zeros(lat_in.shape[1:], jnp.float32)
        pl.semaphore_wait(barrier, 3)

    @pl.when(lat > 0)
    def _():
        pl.semaphore_wait(barrier, 4)

    for copy in loads:
        copy.wait()

    lane = lax.broadcasted_iota(jnp.int32, (SUB, LANE), 1)
    wide_lane = lax.broadcasted_iota(jnp.int32, (SUB, width), 1)
    sub = lax.broadcasted_iota(jnp.int32, (SUB, width), 0)
    slot_of = lane // 4
    early = lax.rem(lane, 4) < 2
    row_base = (lat * rows).astype(jnp.float32) + (sub * run).astype(jnp.float32) + 0.5
    total = rows * lat_n
    cor_base = coriolis_base + row_base * (coriolis_slope / total)

    def rolled(value, shift):
        return pltpu.roll(value, shift % value.shape[1], 1)

    def place(packed, value, i):
        return jnp.where(slot_of == i, rolled(value, 2 + 4 * i)[:, :LANE], packed)

    def unplace(packed, i):
        edge = rolled(packed, LANE - 2 - 4 * i)
        return edge if tiles == 1 else jnp.concatenate([edge] * tiles, axis=1)

    def pair_of(j):
        return lax.rem(j + positions - 1, positions)

    def keep_edges(n, j, first, second):
        lon_out[0, n, j] = jnp.where(early, first, rolled(second, 2))
        lon_out[1, n, j] = jnp.where(early, rolled(first, -2), second)

    def lon_copy(d, n, c):
        part = pl.ds(c * CHUNK, CHUNK)
        return pltpu.make_async_remote_copy(
            src_ref=lon_out.at[d, n, part], dst_ref=lon_in.at[d, n, part],
            send_sem=lon_ssem.at[d, n, c], recv_sem=lon_rsem.at[d, n, c],
            device_id={"lon": east if d == 0 else west}, device_id_type=MESH)

    def lat_copy(src, dst, n, where):
        return pltpu.make_async_remote_copy(
            src_ref=lat_out.at[src, n], dst_ref=lat_in.at[dst, n],
            send_sem=lat_ssem.at[src, n], recv_sem=lat_rsem.at[dst, n],
            device_id=where, device_id_type=MESH)

    def send_lat(n, q):
        for i in range(items):
            for k in range(2):
                lat_out[1, n, pl.ds(2 * i + k, 1)] = q[i, 2 + k, pl.ds(0, 1)]

        @pl.when(lat > 0)
        def _():
            lat_copy(1, 1, n, {"lat": lat - 1}).start()

        @pl.when(lat < lat_n - 1)
        def _():
            for i in range(items):
                for k in range(2):
                    lat_out[0, n, pl.ds(2 * i + k, 1)] = q[i, run + k, pl.ds(SUB - 1, 1)]
            lat_copy(0, 0, n, {"lat": lat + 1}).start()

        @pl.when(lat == lat_n - 1)
        def _():
            for i in range(items):
                for k in range(2):
                    lat_out[0, n, pl.ds(2 * i + k, 1)] = q[i, run + 1 - k, pl.ds(SUB - 1, 1)]
            back = (
                lax.broadcasted_iota(jnp.int32, (width, width), 0)
                + lax.broadcasted_iota(jnp.int32, (width, width), 1)
            ) == width - 1
            line = lax.broadcasted_iota(jnp.int32, (2 * items, width), 0)
            turned = jnp.dot(
                lat_out[0, n], back.astype(jnp.float32),
                precision=lax.Precision.HIGHEST, preferred_element_type=jnp.float32)
            lat_out[0, n] = jnp.where(line < items, turned, -turned)
            lat_copy(0, 1, n, {"lon": mirror}).start()

    def send_chunk(n, c, q):
        lon_copy(0, n, c).start()
        lon_copy(1, n, c).start()

        @pl.when(c == 0)
        def _():
            send_lat(n, q)

    def first_state(c, carry):
        def one(jj, inner):
            j = c * CHUNK + jj
            p = pair_of(j)
            packs = []
            for a in range(2):
                r = 2 * p + a
                packed = jnp.zeros((SUB, LANE), jnp.float32)
                for lv in range(levels):
                    w = [min_[t, lv, pl.ds(r, SUB, stride=run)].astype(jnp.float32) for t in range(tiles)]
                    w = jnp.concatenate(w, axis=1) if tiles > 1 else w[0]
                    wet[lv, r] = w
                    for f in range(FIELDS):
                        i = f * levels + lv
                        x = [fin[t, f, lv, pl.ds(r, SUB, stride=run)] for t in range(tiles)]
                        x = (jnp.concatenate(x, axis=1) if tiles > 1 else x[0]) * w
                        q0[i, r + 2] = x
                        packed = place(packed, x, i)
                packs.append(packed)
            keep_edges(0, j, *packs)
            return inner

        lax.fori_loop(0, CHUNK, one, 0)
        send_chunk(0, c, q0)
        return carry

    lax.fori_loop(0, chunks, first_state, 0)

    def stage(n, qi, qb, qo, base_coef, in_coef, step_coef, last):
        @pl.when(lat > 0)
        def _():
            lat_copy(0, 0, n, {"lat": lat - 1}).wait_recv()

        lat_copy(0, 1, n, {"lon": mirror}).wait_recv()
        for i in range(items):
            for k in range(2):
                south = jnp.broadcast_to(lat_in[0, n, pl.ds(2 * i + k, 1)], (SUB, width))
                north = jnp.broadcast_to(lat_in[1, n, pl.ds(2 * i + k, 1)], (SUB, width))
                qi[i, k] = jnp.where(sub == 0, south, pltpu.roll(qi[i, run + k], 1, 0))
                qi[i, run + 2 + k] = jnp.where(sub == SUB - 1, north, pltpu.roll(qi[i, 2 + k], SUB - 1, 0))

        own = in_coef - 4.0 * spreading_coefficient * step_coef

        def one_row(r, halo):
            cor = cor_base + r.astype(jnp.float32) * (coriolis_slope / total)
            grad_x = jnp.zeros((SUB, width), jnp.float32)
            grad_y = jnp.zeros((SUB, width), jnp.float32)
            packed = jnp.zeros((SUB, LANE), jnp.float32)
            for lv in range(levels):
                gain = wet[lv, r] * step_coef
                u = qi[2 * levels + lv, r + 2]
                v = qi[3 * levels + lv, r + 2]
                un = u * (-1.0 / 12.0)
                vn = v * (-1.0 / 12.0)
                slopes = []
                for f in range(FIELDS):
                    i = f * levels + lv
                    x = qi[i, r + 2]
                    s2, s1, n1, n2 = qi[i, r], qi[i, r + 1], qi[i, r + 3], qi[i, r + 4]
                    edge = unplace(halo, i)
                    w1 = rolled(jnp.where(wide_lane == width - 1, edge, x), 1)
                    w2 = rolled(jnp.where(wide_lane >= width - 2, edge, x), 2)
                    e1 = rolled(jnp.where(wide_lane == 0, edge, x), -1)
                    e2 = rolled(jnp.where(wide_lane <= 1, edge, x), -2)
                    dx = 8.0 * (e1 - w1) - (e2 - w2)
                    dy = 8.0 * (n1 - s1) - (n2 - s2)
                    change = un * dx + vn * dy + spreading_coefficient * ((e1 + w1) + (n1 + s1))
                    slopes.append((dx, dy))
                    if f == 2:
                        kr = gravity * haline_coef / 12.0
                        kt = gravity * thermal_coef / 12.0
                        grad_x = grad_x + (kr * slopes[1][0] - kt * slopes[0][0])
                        grad_y = grad_y + (kr * slopes[1][1] - kt * slopes[0][1])
                        change = change + (cor * v - grad_x)
                    if f == 3:
                        change = change - (cor * u + grad_y)
                    new = own * x + gain * change
                    if base_coef:
                        new = new + base_coef * qb[i, r + 2]
                    if last:
                        for t in range(tiles):
                            fout[t, f, lv, pl.ds(r, SUB, stride=run)] = new[:, t * LANE:(t + 1) * LANE]
                    else:
                        qo[i, r + 2] = new
                        packed = place(packed, new, i)
            return packed

        def chunk(c, carry):
            lon_copy(0, n, c).wait_recv()
            lon_copy(1, n, c).wait_recv()

            def one(jj, inner):
                j = c * CHUNK + jj
                p = pair_of(j)
                from_west = lon_in[0, n, j]
                from_east = lon_in[1, n, j]
                first = one_row(2 * p, jnp.where(early, from_west, rolled(from_east, 2)))
                second = one_row(2 * p + 1, jnp.where(early, rolled(from_west, -2), from_east))
                if not last:
                    keep_edges(n + 1, j, first, second)
                return inner

            lax.fori_loop(0, CHUNK, one, 0)
            if not last:
                send_chunk(n + 1, c, qo)
            return carry

        lax.fori_loop(0, chunks, chunk, 0)

    for step in range(STEPS):
        n = 3 * step
        stage(n, q0, None, q1, 0.0, 1.0, time_step, False)
        stage(n + 1, q1, q0, q2, 0.75, 0.25, 0.25 * time_step, False)
        stage(n + 2, q2, q0, q0, 1.0 / 3.0, 2.0 / 3.0, 2.0 / 3.0 * time_step, step == STEPS - 1)

    stores = []
    for j in range(tiles):
        stores.append(pltpu.make_async_copy(
            fout.at[j], out_hbm.at[:, :, :, pl.ds(j * LANE, LANE)], local_sem.at[2 * j]))
    for copy in stores:
        copy.start()

    def sent(k, carry):
        n = k // chunks
        c = lax.rem(k, chunks)
        lon_copy(0, n, c).wait_send()
        lon_copy(1, n, c).wait_send()
        return carry

    lax.fori_loop(0, 3 * STEPS * chunks, sent, 0)
    for n in range(3 * STEPS):
        lat_copy(0, 1, n, {"lon": mirror}).wait_send()

        @pl.when(lat > 0)
        def _():
            lat_copy(1, 1, n, {"lat": lat - 1}).wait_send()

    for copy in stores:
        copy.wait()


def shards(lon_n, lat_n, ocean_state, sea_mask):
    fields, levels, rows, width = ocean_state.shape
    items = fields * levels
    run = rows // SUB
    tiles = width // LANE
    stages = 3 * STEPS
    positions = run // 2
    chunks = positions // CHUNK
    f32 = jnp.float32
    state = pltpu.VMEM((items, run + 4, SUB, width), f32)
    return pl.pallas_call(
        functools.partial(kernel, levels, rows, width, lon_n, lat_n),
        out_shape=jax.ShapeDtypeStruct(ocean_state.shape, f32),
        in_specs=[pl.BlockSpec(memory_space=pl.ANY)] * 2,
        out_specs=pl.BlockSpec(memory_space=pl.ANY),
        scratch_shapes=[
            pltpu.VMEM((tiles, fields, levels, rows, LANE), f32),
            pltpu.VMEM((tiles, levels, rows, LANE), jnp.int32),
            pltpu.VMEM((tiles, fields, levels, rows, LANE), f32),
            pltpu.VMEM((levels, run, SUB, width), f32),
            state, state, state,
            pltpu.VMEM((2, stages, positions, SUB, LANE), f32),
            pltpu.VMEM((2, stages, positions, SUB, LANE), f32),
            pltpu.VMEM((2, stages, 2 * items, width), f32),
            pltpu.VMEM((2, stages, 2 * items, width), f32),
            pltpu.SemaphoreType.DMA((2 * tiles,)),
            pltpu.SemaphoreType.DMA((2, stages, chunks)),
            pltpu.SemaphoreType.DMA((2, stages, chunks)),
            pltpu.SemaphoreType.DMA((2, stages)),
            pltpu.SemaphoreType.DMA((2, stages)),
        ],
        compiler_params=pltpu.CompilerParams(
            collective_id=0, has_side_effects=True, vmem_limit_bytes=56 * 2**20),
    )(ocean_state, sea_mask)


def solution(mesh):
    in_specs = (P(None, None, "lat", "lon"), P(None, "lat", "lon"))
    out_specs = P(None, None, "lat", "lon")
    body = functools.partial(shards, mesh.shape["lon"], mesh.shape["lat"])
    return jax.shard_map(body, mesh=mesh, in_specs=in_specs, out_specs=out_specs, check_vma=False)
```

time: 310 us -> 66.2 us (0.21); the launches traced: 305 us -> 66.1 us
  local copies, waits for them, and re-layouts: 99.3 us -> 3.3 us
  other arithmetic: 95.4 us -> 0 us
  Pallas kernels: 0 us -> 62.8 us
  waiting for transfers between devices: 58.9 us -> 0 us
  starting transfers between devices: 50.7 us -> 0 us
    pallas_call x0 -> x1, Pallas kernels: none -> 62.8 us  [shards(): pl.pallas_call(functools.partial(kernel, levels, rows, width, lon_n, lat_...]
    ppermute x42 -> x0, waiting for transfers between devices: 58.9 us -> none  [the longest x18 58.8 us: partner(): return lax.ppermute(value, axis, pairs)]
    slice x18 -> x0, local copies, waits for them, and re-layouts: 53.9 us -> none  [the longest x12 35.9 us: extended(): lax.slice_in_dim(cells, cells.shape[dim] - width, cells.shape[dim], axis=...]
    ppermute x42 -> x0, starting transfers between devices: 50.7 us -> none  [the longest x12 35.5 us: extended(): lax.ppermute(head, axis, [((i + 1) % count, i) for i in range(count)])]
    another operation x30 -> x0, other arithmetic: 44.7 us -> none  [the longest x24 43 us: full_tendency(): jnp.stack([heat_increment, brine_increment, eastward_gradient, northward_...]
    ppermute x12 -> x0, local copies, waits for them, and re-layouts: 32.4 us -> none  [the longest x6 16.2 us: extended(): lax.ppermute(head, axis, [((i + 1) % count, i) for i in range(count)])]
    concatenate x6 -> x0, other arithmetic: 25 us -> none  [close_rows(): jnp.concatenate([lower, bordered_grid_values[:, :, 2:-2, :], upper], axis=2)]
    slice x6 -> x0, other arithmetic: 10.2 us -> none  [extended(): lax.slice_in_dim(cells, cells.shape[dim] - width, cells.shape[dim], axis=...]
  transfers between devices with their start and end apart: 42 -> 0, of which waited for: 18 -> 0; matrix products, arithmetic and copies ran while one was open for 14% -> 0% of each run, Pallas kernels for 0% -> 0%
where the time goes in v1:
time: 66.2 us; the launch traced here: 66.1 us
  Pallas kernels  62.8 us (95%)
  local copies, waits for them, and re-layouts  3.3 us (5%)
    pallas_call x1, Pallas kernels, shards(): pl.pallas_call(functools.partial(kernel, levels, rows, width, lon_n, lat_...  62.8 us
    unnamed x1, local copies, waits for them, and re-layouts  3.3 us

profile of v1, /device:TPU:0, one launch (start us, length us, event | category | flops | bytes accessed | tf_op | source)
XLA Modules:
  0.0 66.1 jit_solution(2391125081340638099)
XLA Ops:
  0.0 62.8 %shard_map.28 = f32[4,6,192,128]{3,2,1,0:T(8,128)} custom-call(f32[4,6,192,128]{3,2,1,0:T(8,128)} %in_hbm.1, s32[6,192,128]{2,1,0:T(8,128)} %mask_hbm.1), custom_call_target="tpu_custom_call" | custom-call | tf_op jit(solution)/shard_map/pallas_call | solution.py:311
  62.8 3.3 %copy.4 = f32[4,6,192,128]{3,2,1,0:T(8,128)} copy(f32[4,6,192,128]{3,2,1,0:T(8,128)} %shard_map.28) | data formatting | bytes 4718592

commit v2 on v1

--- a/solution.py
+++ b/solution.py
@@ -28,6 +28,7 @@
     levels, rows, width, lon_n, lat_n,
     in_hbm, mask_hbm, out_hbm,
     fin, min_, fout, wet, q0, q1, q2,
+    weight, edge_weight, only, left, edge_left, found,
     lon_out, lon_in, lat_out, lat_in,
     local_sem, lon_ssem, lon_rsem, lat_ssem, lat_rsem,
 ):
@@ -79,7 +80,6 @@
         copy.wait()
 
     lane = lax.broadcasted_iota(jnp.int32, (SUB, LANE), 1)
-    wide_lane = lax.broadcasted_iota(jnp.int32, (SUB, width), 1)
     sub = lax.broadcasted_iota(jnp.int32, (SUB, width), 0)
     slot_of = lane // 4
     early = lax.rem(lane, 4) < 2
@@ -93,9 +93,29 @@
     def place(packed, value, i):
         return jnp.where(slot_of == i, rolled(value, 2 + 4 * i)[:, :LANE], packed)
 
-    def unplace(packed, i):
-        edge = rolled(packed, LANE - 2 - 4 * i)
-        return edge if tiles == 1 else jnp.concatenate([edge] * tiles, axis=1)
+    def taps(source, shape):
+        column = lax.broadcasted_iota(jnp.int32, shape, 1)
+        d = source - lax.rem(column, width)
+
+        def at(k):
+            return (d == k).astype(jnp.float32)
+
+        return jnp.where(
+            column < width, 8.0 * (at(1) - at(-1)) - (at(2) - at(-2)), at(1) + at(-1)
+        ).astype(jnp.bfloat16)
+
+    shape = (2 * width, 2 * width)
+    weight[...] = taps(lax.rem(lax.broadcasted_iota(jnp.int32, shape, 0), width), shape)
+    shape = (2 * LANE, 2 * width)
+    line = lax.rem(lax.broadcasted_iota(jnp.int32, shape, 0), 4)
+    edge_weight[...] = taps(jnp.where(line < 2, line - 2, line - 2 + width), shape)
+    slot_two = lax.broadcasted_iota(jnp.int32, (2 * SUB, LANE), 1) // 4
+    for i in range(items):
+        only[i] = (slot_two == i).astype(jnp.float32).astype(jnp.bfloat16)
+
+    def split(value):
+        high = value.astype(jnp.bfloat16)
+        return high, (value - high.astype(jnp.float32)).astype(jnp.bfloat16)
 
     def pair_of(j):
         return lax.rem(j + positions - 1, positions)
@@ -200,7 +220,7 @@
 
         own = in_coef - 4.0 * spreading_coefficient * step_coef
 
-        def one_row(r, halo):
+        def one_row(r, a):
             cor = cor_base + r.astype(jnp.float32) * (coriolis_slope / total)
             grad_x = jnp.zeros((SUB, width), jnp.float32)
             grad_y = jnp.zeros((SUB, width), jnp.float32)
@@ -216,14 +236,11 @@
                     i = f * levels + lv
                     x = qi[i, r + 2]
                     s2, s1, n1, n2 = qi[i, r], qi[i, r + 1], qi[i, r + 3], qi[i, r + 4]
-                    edge = unplace(halo, i)
-                    w1 = rolled(jnp.where(wide_lane == width - 1, edge, x), 1)
-                    w2 = rolled(jnp.where(wide_lane >= width - 2, edge, x), 2)
-                    e1 = rolled(jnp.where(wide_lane == 0, edge, x), -1)
-                    e2 = rolled(jnp.where(wide_lane <= 1, edge, x), -2)
-                    dx = 8.0 * (e1 - w1) - (e2 - w2)
+                    line = pl.ds(i * 2 * SUB + a * SUB, SUB)
+                    dx = found[line, pl.ds(0, width)]
+                    sides = found[line, pl.ds(width, width)]
                     dy = 8.0 * (n1 - s1) - (n2 - s2)
-                    change = un * dx + vn * dy + spreading_coefficient * ((e1 + w1) + (n1 + s1))
+                    change = un * dx + vn * dy + spreading_coefficient * (sides + (n1 + s1))
                     slopes.append((dx, dy))
                     if f == 2:
                         kr = gravity * haline_coef / 12.0
@@ -253,8 +270,22 @@
                 p = pair_of(j)
                 from_west = lon_in[0, n, j]
                 from_east = lon_in[1, n, j]
-                first = one_row(2 * p, jnp.where(early, from_west, rolled(from_east, 2)))
-                second = one_row(2 * p + 1, jnp.where(early, rolled(from_west, -2), from_east))
+                halo = jnp.concatenate([
+                    jnp.where(early, from_west, rolled(from_east, 2)),
+                    jnp.where(early, rolled(from_west, -2), from_east)], axis=0)
+                halo_high, halo_low = split(halo)
+                for i in range(items):
+                    lines = pl.ds(i * 2 * SUB, 2 * SUB)
+                    high, low = split(qi[i, pl.ds(2 * p + 2, 2)].reshape(2 * SUB, width))
+                    left[lines, pl.ds(0, width)] = high
+                    left[lines, pl.ds(width, width)] = low
+                    edge_left[lines, pl.ds(0, LANE)] = halo_high * only[i]
+                    edge_left[lines, pl.ds(LANE, LANE)] = halo_low * only[i]
+                found[...] = jnp.dot(
+                    left[...], weight[...], preferred_element_type=jnp.float32
+                ) + jnp.dot(edge_left[...], edge_weight[...], preferred_element_type=jnp.float32)
+                first = one_row(2 * p, 0)
+                second = one_row(2 * p + 1, 1)
                 if not last:
                     keep_edges(n + 1, j, first, second)
                 return inner
@@ -319,6 +350,12 @@
             pltpu.VMEM((tiles, fields, levels, rows, LANE), f32),
             pltpu.VMEM((levels, run, SUB, width), f32),
             state, state, state,
+            pltpu.VMEM((2 * width, 2 * width), jnp.bfloat16),
+            pltpu.VMEM((2 * LANE, 2 * width), jnp.bfloat16),
+            pltpu.VMEM((items, 2 * SUB, LANE), jnp.bfloat16),
+            pltpu.VMEM((items * 2 * SUB, 2 * width), jnp.bfloat16),
+            pltpu.VMEM((items * 2 * SUB, 2 * LANE), jnp.bfloat16),
+            pltpu.VMEM((items * 2 * SUB, 2 * width), f32),
             pltpu.VMEM((2, stages, positions, SUB, LANE), f32),
             pltpu.VMEM((2, stages, positions, SUB, LANE), f32),
             pltpu.VMEM((2, stages, 2 * items, width), f32),

time: 66.2 us -> 50.6 us (0.76)
  Pallas kernels: 62.8 us -> 47.1 us
    pallas_call x1, Pallas kernels: 62.8 us -> 47.1 us  [shards(): pl.pallas_call(functools.partial(kernel, levels, rows, width, lon_n, lat_...]
where the time goes in v2:
time: 50.6 us; the launch traced here: 50.4 us
  Pallas kernels  47.1 us (93%)
  local copies, waits for them, and re-layouts  3.3 us (7%)
    pallas_call x1, Pallas kernels, shards(): pl.pallas_call(functools.partial(kernel, levels, rows, width, lon_n, lat_...  47.1 us
    unnamed x1, local copies, waits for them, and re-layouts  3.3 us

profile of v2, /device:TPU:0, one launch (start us, length us, event | category | flops | bytes accessed | tf_op | source)
XLA Modules:
  0.0 50.4 jit_solution(8143627743170130823)
XLA Ops:
  0.0 47.1 %shard_map.28 = f32[4,6,192,128]{3,2,1,0:T(8,128)} custom-call(f32[4,6,192,128]{3,2,1,0:T(8,128)} %in_hbm.1, s32[6,192,128]{2,1,0:T(8,128)} %mask_hbm.1), custom_call_target="tpu_custom_call" | custom-call | tf_op jit(solution)/shard_map/pallas_call | solution.py:342
  47.1 3.3 %copy.4 = f32[4,6,192,128]{3,2,1,0:T(8,128)} copy(f32[4,6,192,128]{3,2,1,0:T(8,128)} %shard_map.28) | data formatting | bytes 4718592
